TPU v7x, 256 devices: a whole 4x4x8 slice. The times are simulated.
256 devices in a mesh: dom: 32 (over y, x, core), blk: 8 (over z).
Axes of the slice: x: 4, y: 4, z: 8, core: 2. Of those that a mesh axis runs over, the one named last changes fastest.
Arguments:
- source: bfloat16 [4096, 192], P(('dom', 'blk')), may hold values from -6 to 6
- lam_init: bfloat16 [4096, 192], P(('dom', 'blk')), may hold values from -6 to 6
- offd: bfloat16 [4096, 192, 1152], P(('dom', 'blk')), may hold values from -0.1875 to 0.1875
- dinv: bfloat16 [192, 786432], P(None, ('dom', 'blk')), may hold values from -0.4375 to 0.4375
- colidx: int32 [4096, 6], P(('dom', 'blk')), may hold values from 0 to 191
- face_list: int32 [32, 64], P('dom'), may hold values from 0 to 127
- partner: int32 [32], P('dom'), may hold values from 0 to 31, as said below
- perf_block: int32 [32768], P(('dom', 'blk')), may hold values from 0 to 15
- perf_well: int32 [32768], P(('dom', 'blk')), may hold values from 0 to 63
- perf_sens: bfloat16 [32768, 192], P(('dom', 'blk')), may hold values from -0.21875 to 0.21875
- obj_weight: float32 [1024], replicated, may hold values from 0.5 to 2
- step_index: int32 [1], replicated, may hold values from 0 to 1023
Outputs:
- adjoint: float32 [4096, 192], P(('dom', 'blk'))
- control_grad: float32 [2048], P(('dom', 'blk'))
Inputs may be any that keep to these rules, and one draw needn't show every extreme that they name: Below 128 an own block of the partition, from 128 on halo block colidx - 128. `face_list`: blocks of the partition's own 128, repeats possible. A pairing: partner[p] != p and partner[partner[p]] == p.
All inputs are finite; a program needn't handle non-finite values.
Results may differ from a plain program's by a relative error of at most 0.0054.
Values may be sent and summed in bfloat16 or wider, within the bound.
No kernel may reach another device: no remote copies, remote signals or barrier semaphores. Data moves between devices by JAX's collectives and lax.ppermute only.
A program may use at most 64 MiB of HBM per device.

v0:
```python
import jax
import jax.numpy as jnp
from jax import lax
from jax.sharding import PartitionSpec as P

WP = 64


def cross_partition(face_rows, partner_id):
    slot_count = lax.axis_size("dom")
    onehot = (jnp.arange(slot_count, dtype=jnp.int32) == partner_id).astype(jnp.bfloat16)
    outgoing = onehot[:, None, None] * face_rows[None, :, :]
    incoming = lax.all_to_all(outgoing, "dom", split_axis=0, concat_axis=0, tiled=True)
    halo_blocks = lax.dynamic_index_in_dim(incoming, partner_id, 0, keepdims=False)
    return halo_blocks


def extended_state(state, face_index, partner_id):
    partition = lax.all_gather(state, "blk", axis=0, tiled=True)
    halo_blocks = cross_partition(partition[face_index], partner_id)
    return jnp.concatenate([partition, halo_blocks], axis=0)


def sweep_once(state, forcing, offd, inverses, colidx, face_index, partner_id):
    extended = extended_state(state, face_index, partner_id)
    picked = extended[colidx].reshape(colidx.shape[0], -1)
    coupled = jnp.einsum("bim,bm->bi", offd, picked, preferred_element_type=jnp.float32)
    residual_rhs = (forcing - coupled).astype(jnp.bfloat16)
    return jnp.einsum("ibj,bj->bi", inverses, residual_rhs, preferred_element_type=jnp.float32)


def body(
    source,
    lam_init,
    offd,
    dinv,
    colidx,
    face_list,
    partner,
    perf_block,
    perf_well,
    perf_sens,
    obj_weight,
    step_index,
):
    weight = lax.dynamic_index_in_dim(obj_weight, step_index[0], 0, keepdims=False)
    forcing = weight * source.astype(jnp.float32)
    width = source.shape[1]
    inverses = dinv.reshape(width, source.shape[0], width)
    face_index = face_list[0]
    partner_id = partner[0]
    first_pass = sweep_once(
        lam_init, forcing, offd, inverses, colidx, face_index, partner_id
    ).astype(jnp.bfloat16)
    adjoint = sweep_once(first_pass, forcing, offd, inverses, colidx, face_index, partner_id)
    contrib = jnp.sum(perf_sens.astype(jnp.float32) * adjoint[perf_block], axis=1)
    onehot = (perf_well[:, None] == jnp.arange(WP, dtype=jnp.int32)[None, :]).astype(jnp.float32)
    well_terms = -jnp.dot(contrib, onehot, precision=lax.Precision.HIGHEST)
    control_grad = lax.psum_scatter(well_terms, "blk", scatter_dimension=0, tiled=True)
    return (adjoint, control_grad)


def solution(mesh):
    placed = (
        P(("dom", "blk"), None),
        P(("dom", "blk"), None),
        P(("dom", "blk"), None, None),
        P(None, ("dom", "blk")),
        P(("dom", "blk"), None),
        P("dom", None),
        P("dom"),
        P(("dom", "blk")),
        P(("dom", "blk")),
        P(("dom", "blk"), None),
        P(),
        P(),
    )
    return jax.shard_map(
        body,
        mesh=mesh,
        in_specs=placed,
        out_specs=(P(("dom", "blk"), None), P(("dom", "blk"))),
        check_vma=False,
    )
```

profile of v0, /device:TPU:2, one launch (start us, length us, event | category | flops | bytes accessed | tf_op | source)
XLA Modules:
  0.0 136.8 jit_solution(17076358415785166185)
XLA Ops:
  1.3 28.4 %all_gather.6 = bf16[128,192]{1,0:T(8,128)(2,1)S(1)} all-gather(bf16[16,192]{1,0:T(8,128)(2,1)} %param.13), channel_id=1, replica_groups=mesh['dom'=32,'blk'=8] {'blk'}, dimensions={0}, use_global_device_ids=true | all-gather | bytes 55296 | tf_op jit(solution)/shard_map/all_gather | solution.py:19
  29.7 0.7 fusion.10
  30.3 0.7 gather_fusion
  31.0 0.0 copy-start.4
  31.1 0.0 copy-start.1
  31.1 1.2 broadcast_multiply_fusion.1
  32.2 7.7 %all-to-all-start = ((bf16[32,64,192]{2,1,0:T(8,128)(2,1)}), bf16[32,64,192]{2,1,0:T(8,128)(2,1)}, u32[]{:S(2)}, u32[]{:S(2)}) async-start(bf16[32,64,192]{2,1,0:T(8,128)(2,1)} %broadcast_multiply_fusion.1), calls=%async_computation | async-start | bytes 2097152 | tf_op jit(solution)/shard_map/all_to_all | solution.py:13
  39.9 0.0 copy-done.4
  40.0 0.1 copy.18
  40.0 0.1 reshape.62
  40.8 0.0 copy-done.1
  40.8 0.7 copy.29
  41.5 1.3 dynamic_slice.11
  42.8 13.3 %all-to-all-done = bf16[32,64,192]{2,1,0:T(8,128)(2,1)} async-done(((bf16[32,64,192]{2,1,0:T(8,128)(2,1)}), bf16[32,64,192]{2,1,0:T(8,128)(2,1)}, u32[]{:S(2)}, u32[]{:S(2)}) %all-to-all-start) | async-done | bytes 786464 | tf_op jit(solution)/shard_map/all_to_all | solution.py:13
  56.1 0.8 dynamic-slice_bitcast_fusion.1
  56.9 0.8 gather_fusion.1
  57.7 0.1 reshape.110
  57.8 0.0 copy-start.3
  57.8 5.2 %fusion.12 = f32[16,1,192]{2,1,0:T(1,128)S(1)} fusion(bf16[16,1152,1]{1,2,0:T(2,128)(2,1)S(1)} %reshape.110, bf16[16,192,1152]{2,1,0:T(8,128)(2,1)} %param.14), kind=kOutput, calls=%fused_computation.38 | convolution fusion | flops 7077888 | bytes 7127040 | tf_op jit(solution)/shard_map/bim,bm->bi/dot_general | solution.py:27
  62.9 0.0 copy-done.3
  62.9 0.7 fusion.8
  63.6 0.3 fusion.6
  63.9 24.6 %all_gather.7 = bf16[128,192]{1,0:T(8,128)(2,1)S(1)} all-gather(bf16[16,192]{1,0:T(8,128)(2,1)S(1)} %bitcast.59), channel_id=1, replica_groups=mesh['dom'=32,'blk'=8] {'blk'}, dimensions={0}, use_global_device_ids=true | all-gather | bytes 55296 | tf_op jit(solution)/shard_map/all_gather | solution.py:19
  88.5 0.7 gather_fusion.2
  89.2 0.0 copy-start.2
  89.2 0.0 copy-start.7
  89.2 0.0 copy-start.5
  89.2 1.1 broadcast_multiply_fusion
  90.3 5.0 %all-to-all-start.1 = ((bf16[32,64,192]{2,1,0:T(8,128)(2,1)}), bf16[32,64,192]{2,1,0:T(8,128)(2,1)S(1)}, u32[]{:S(2)}, u32[]{:S(2)}) async-start(bf16[32,64,192]{2,1,0:T(8,128)(2,1)} %broadcast_multiply_fusion), calls=%async_computation.1 | async-start | bytes 2097152 | tf_op jit(solution)/shard_map/all_to_all | solution.py:13
  95.4 0.0 copy-done.2
  95.4 0.1 copy.19
  95.5 0.0 copy-done.7
  95.5 0.6 dynamic-slice
  96.8 0.0 copy-done.5
  96.8 14.8 %all-to-all-done.1 = bf16[32,64,192]{2,1,0:T(8,128)(2,1)S(1)} async-done(((bf16[32,64,192]{2,1,0:T(8,128)(2,1)}), bf16[32,64,192]{2,1,0:T(8,128)(2,1)S(1)}, u32[]{:S(2)}, u32[]{:S(2)}) %all-to-all-start.1) | async-done | bytes 786464 | tf_op jit(solution)/shard_map/all_to_all | solution.py:13
  111.6 0.8 gather_fusion.3
  112.4 0.1 reshape.112
  112.5 5.2 %fusion.13 = f32[16,1,192]{2,1,0:T(1,128)S(1)} fusion(bf16[16,1152,1]{1,2,0:T(2,128)(2,1)S(1)} %reshape.112, bf16[16,192,1152]{2,1,0:T(8,128)(2,1)} %param.14), kind=kOutput, calls=%fused_computation.39 | convolution fusion | flops 7077888 | bytes 7127040 | tf_op jit(solution)/shard_map/bim,bm->bi/dot_general | solution.py:27
  117.7 0.0 copy-start.6
  117.7 0.7 fusion.9
  118.4 0.3 fusion.4
  118.7 0.0 copy-start
  118.7 0.8 gather_fusion.4
  119.5 0.1 multiply_reduce_fusion
  119.6 0.0 copy-done.6
  119.6 0.2 fusion
  119.8 16.4 %all-reduce = f32[64]{0:T(128)S(1)} all-reduce(f32[64]{0:T(128)S(1)} %fusion), channel_id=2, replica_groups=mesh['dom'=32,'blk'=8] {'blk'}, use_global_device_ids=true, to_apply=%region_1.2.clone | all-reduce | flops 64 | bytes 512
  136.2 0.6 dynamic-slice.1
  136.8 0.0 copy-done
  (11 shorter events, 0.1 us)
Async XLA Ops:
  31.0 8.9 %copy-start.4 = (s32[16,6]{0,1:T(8,128)S(1)}, s32[16,6]{0,1:T(8,128)}, u32[]{:S(2)}) copy-start(s32[16,6]{0,1:T(8,128)} %param.16) | copy-start | bytes 1156
  31.1 9.7 %copy-start.1 = (bf16[192,3072]{1,0:T(8,128)(2,1)S(1)}, bf16[192,3072]{1,0:T(8,128)(2,1)}, u32[]{:S(2)}) copy-start(bf16[192,3072]{1,0:T(8,128)(2,1)} %param.15) | copy-start | bytes 3538948
  32.2 23.8 %all-to-all-start = ((bf16[32,64,192]{2,1,0:T(8,128)(2,1)}), bf16[32,64,192]{2,1,0:T(8,128)(2,1)}, u32[]{:S(2)}, u32[]{:S(2)}) async-start(bf16[32,64,192]{2,1,0:T(8,128)(2,1)} %broadcast_multiply_fusion.1), calls=%async_computation | async-start | bytes 2097152 | tf_op jit(solution)/shard_map/all_to_all | solution.py:13
  57.8 5.2 %copy-start.3 = (bf16[16,192]{1,0:T(8,128)(2,1)S(1)}, bf16[16,192]{1,0:T(8,128)(2,1)}, u32[]{:S(2)}) copy-start(bf16[16,192]{1,0:T(8,128)(2,1)} %param.12) | copy-start | bytes 18436
  89.2 6.2 %copy-start.2 = (bf16[128,192]{0,1:T(8,128)(2,1)S(1)}, bf16[128,192]{0,1:T(8,128)(2,1)}, u32[]{:S(2)}) copy-start(bf16[128,192]{0,1:T(8,128)(2,1)} %param.21) | copy-start | bytes 147460
  89.2 6.3 %copy-start.7 = (u32[256]{0:T(256)S(1)}, u32[256]{0:T(256)}, u32[]{:S(2)}) copy-start(u32[256]{0:T(256)} %constant.35) | copy-start | bytes 3076
  89.2 7.6 %copy-start.5 = (s32[128]{0:T(128)S(1)}, s32[128]{0:T(128)}, u32[]{:S(2)}) copy-start(s32[128]{0:T(128)} %param.19) | copy-start | bytes 1540
  90.3 21.3 %all-to-all-start.1 = ((bf16[32,64,192]{2,1,0:T(8,128)(2,1)}), bf16[32,64,192]{2,1,0:T(8,128)(2,1)S(1)}, u32[]{:S(2)}, u32[]{:S(2)}) async-start(bf16[32,64,192]{2,1,0:T(8,128)(2,1)} %broadcast_multiply_fusion), calls=%async_computation.1 | async-start | bytes 2097152 | tf_op jit(solution)/shard_map/all_to_all | solution.py:13
  117.7 1.9 %copy-start.6 = (s32[128]{0:T(128)S(1)}, s32[128]{0:T(128)}, u32[]{:S(2)}) copy-start(s32[128]{0:T(128)} %param.20) | copy-start | bytes 1540
  118.7 18.1 %copy-start = (f32[16,1,192]{2,0,1:T(8,128)}, f32[16,1,192]{2,0,1:T(8,128)S(1)}, u32[]{:S(2)}) copy-start(f32[16,1,192]{2,0,1:T(8,128)S(1)} %copy.43) | copy-start | bytes 36868
where the time goes:
time: 137 us
  blocking collectives  69.3 us (51%)
  waiting for transfers between devices  28.1 us (21%)
  starting transfers between devices  12.7 us (9%)
  matrix products  11.1 us (8%)
  local copies, waits for them, and re-layouts  8.15 us (6%)
  other arithmetic  4.47 us (3%)
  between operations  2.83 us (2%)
    all_gather x2, blocking collectives, extended_state(): partition = lax.all_gather(state, 'blk', axis=0, tiled=True)  52.9 us
    all_to_all x2, waiting for transfers between devices, cross_partition(): lax.all_to_all(outgoing, 'dom', split_axis=0, concat_axis=0, tiled=True)  28.1 us
    unnamed x1, blocking collectives  16.4 us
    all_to_all x2, starting transfers between devices, cross_partition(): lax.all_to_all(outgoing, 'dom', split_axis=0, concat_axis=0, tiled=True)  12.7 us
    dot_general x2, matrix products, sweep_once(): jnp.einsum('bim,bm->bi', offd, picked, preferred_element_type=jnp.float32)  10.3 us
  transfers between devices with their start and end apart: 2, of which 2 were waited for; matrix products, arithmetic and copies ran while one was open for 2% of the time, Pallas kernels for 0%

commit v1 on v0

--- a/solution.py
+++ b/solution.py
@@ -4,6 +4,22 @@
 from jax.sharding import PartitionSpec as P
 
 WP = 64
+
+
+def collect(x, axis, dim):
+    ways, here, step = (lax.axis_size(axis), lax.axis_index(axis), x.shape[dim])
+    shape = [n * ways if d == dim else n for d, n in enumerate(x.shape)]
+    full = lax.dynamic_update_slice_in_dim(jnp.zeros(shape, x.dtype), x, here * step, axis=dim)
+    going_up = going_down = x
+    for far in range(1, ways // 2 + 1):
+        going_up = lax.ppermute(going_up, axis, [(d, (d + 1) % ways) for d in range(ways)])
+        full = lax.dynamic_update_slice_in_dim(full, going_up, (here - far) % ways * step, axis=dim)
+        if 2 * far < ways:
+            going_down = lax.ppermute(going_down, axis, [(d, (d - 1) % ways) for d in range(ways)])
+            full = lax.dynamic_update_slice_in_dim(
+                full, going_down, (here + far) % ways * step, axis=dim
+            )
+    return full
 
 
 def cross_partition(face_rows, partner_id):
@@ -16,7 +32,7 @@
 
 
 def extended_state(state, face_index, partner_id):
-    partition = lax.all_gather(state, "blk", axis=0, tiled=True)
+    partition = collect(state, "blk", 0)
     halo_blocks = cross_partition(partition[face_index], partner_id)
     return jnp.concatenate([partition, halo_blocks], axis=0)
 

time: 137 us -> 124 us (0.905)
  blocking collectives: 69.3 us -> 14.2 us
  starting transfers between devices: 12.7 us -> 35.1 us
  waiting for transfers between devices: 28.1 us -> 45.9 us
    all_gather x2 -> x0, blocking collectives: 52.9 us -> none  [extended_state(): partition = lax.all_gather(state, 'blk', axis=0, tiled=True)]
    ppermute x0 -> x14, starting transfers between devices: none -> 22.3 us  [the longest x6 20.2 us: collect(): lax.ppermute(going_down, axis, [(d, (d - 1) % ways) for d in range(ways)])]
    ppermute x0 -> x14, waiting for transfers between devices: none -> 17.8 us  [the longest x8 17.8 us: collect(): lax.ppermute(going_up, axis, [(d, (d + 1) % ways) for d in range(ways)])]
    unnamed x1, blocking collectives: 16.4 us -> 14.2 us
  transfers between devices with their start and end apart: 2 -> 16, of which waited for: 2 -> 9; matrix products, arithmetic and copies ran while one was open for 2% -> 3% of each run, Pallas kernels for 0% -> 0%
where the time goes in v1:
time: 124 us; the launch traced here: 123 us
  waiting for transfers between devices  45.9 us (37%)
  starting transfers between devices  35.1 us (28%)
  blocking collectives  14.2 us (11%)
  matrix products  11.1 us (9%)
  local copies, waits for them, and re-layouts  8.91 us (7%)
  other arithmetic  4.42 us (4%)
  between operations  2.92 us (2%)
    all_to_all x2, waiting for transfers between devices, cross_partition(): lax.all_to_all(outgoing, 'dom', split_axis=0, concat_axis=0, tiled=True)  28.1 us
    ppermute x6, starting transfers between devices, collect(): lax.ppermute(going_down, axis, [(d, (d - 1) % ways) for d in range(ways)])  20.2 us
    ppermute x8, waiting for transfers between devices, collect(): lax.ppermute(going_up, axis, [(d, (d + 1) % ways) for d in range(ways)])  17.8 us
    unnamed x1, blocking collectives  14.2 us
    all_to_all x2, starting transfers between devices, cross_partition(): lax.all_to_all(outgoing, 'dom', split_axis=0, concat_axis=0, tiled=True)  12.7 us
    dot_general x2, matrix products, sweep_once(): jnp.einsum('bim,bm->bi', offd, picked, preferred_element_type=jnp.float32)  10.3 us
  transfers between devices with their start and end apart: 16, of which 9 were waited for; matrix products, arithmetic and copies ran while one was open for 3% of the time, Pallas kernels for 0%

profile of v1, /device:TPU:2, one launch (start us, length us, event | category | flops | bytes accessed | tf_op | source)
XLA Modules:
  0.0 122.5 jit_solution(13760470923677630754)
XLA Ops:
  0.6 2.0 %collective-permute-start = (bf16[16,192]{1,0:T(8,128)(2,1)}, bf16[16,192]{1,0:T(8,128)(2,1)S(1)}, u32[]{:S(2)}, u32[]{:S(2)}) collective-permute-start(bf16[16,192]{1,0:T(8,128)(2,1)} %param.13), channel_id=1, source_target_pairs={{0,1},{1,2},{2,3},{3,4},{4,5},{5,6},{6,7},{7,0},{8,9},{9,10},{10,1... | collective-permute-start | bytes 18440 | tf_op jit(solution)/shard_map/ppermute | solution.py:15
  2.6 4.0 %collective-permute-start.1 = (bf16[16,192]{1,0:T(8,128)(2,1)}, bf16[16,192]{1,0:T(8,128)(2,1)S(1)}, u32[]{:S(2)}, u32[]{:S(2)}) collective-permute-start(bf16[16,192]{1,0:T(8,128)(2,1)} %param.13), channel_id=1, source_target_pairs={{0,7},{1,0},{2,1},{3,2},{4,3},{5,4},{6,5},{7,6},{8,15},{9,8},{10,9... | collective-permute-start | bytes 18440 | tf_op jit(solution)/shard_map/ppermute | solution.py:18
  6.7 0.7 fusion.10
  8.0 0.7 constant_dynamic-update-slice_fusion.15
  8.7 0.0 collective-permute-done
  8.7 0.1 collective-permute-start.2
  8.8 0.0 collective-permute-done.1
  8.8 3.2 %collective-permute-start.3 = (bf16[16,192]{1,0:T(8,128)(2,1)S(1)}, bf16[16,192]{1,0:T(8,128)(2,1)S(1)}, u32[]{:S(2)}, u32[]{:S(2)}) collective-permute-start(bf16[16,192]{1,0:T(8,128)(2,1)S(1)} %collective-permute-done.1), channel_id=1, source_target_pairs={{0,7},{1,0},{2,1},{3,2},{4,3},{5,4},{6,5},{7,6},{8,15},{9,8},{10,9... | collective-permute-start | bytes 18440 | tf_op jit(solution)/shard_map/ppermute | solution.py:18
  12.0 1.6 %collective-permute-done.2 = bf16[16,192]{1,0:T(8,128)(2,1)S(1)} collective-permute-done((bf16[16,192]{1,0:T(8,128)(2,1)S(1)}, bf16[16,192]{1,0:T(8,128)(2,1)S(1)}, u32[]{:S(2)}, u32[]{:S(2)}) %collective-permute-start.2) | collective-permute-done | bytes 6176 | tf_op jit(solution)/shard_map/ppermute | solution.py:15
  13.6 0.0 collective-permute-start.4
  13.6 0.0 collective-permute-done.3
  13.6 3.2 %collective-permute-start.5 = (bf16[16,192]{1,0:T(8,128)(2,1)S(1)}, bf16[16,192]{1,0:T(8,128)(2,1)S(1)}, u32[]{:S(2)}, u32[]{:S(2)}) collective-permute-start(bf16[16,192]{1,0:T(8,128)(2,1)S(1)} %collective-permute-done.3), channel_id=1, source_target_pairs={{0,7},{1,0},{2,1},{3,2},{4,3},{5,4},{6,5},{7,6},{8,15},{9,8},{10,9... | collective-permute-start | bytes 18440 | tf_op jit(solution)/shard_map/ppermute | solution.py:18
  16.9 1.6 %collective-permute-done.4 = bf16[16,192]{1,0:T(8,128)(2,1)S(1)} collective-permute-done((bf16[16,192]{1,0:T(8,128)(2,1)S(1)}, bf16[16,192]{1,0:T(8,128)(2,1)S(1)}, u32[]{:S(2)}, u32[]{:S(2)}) %collective-permute-start.4) | collective-permute-done | bytes 6176 | tf_op jit(solution)/shard_map/ppermute | solution.py:15
  18.5 0.0 collective-permute-start.6
  18.5 4.8 %collective-permute-done.6 = bf16[16,192]{1,0:T(8,128)(2,1)S(1)} collective-permute-done((bf16[16,192]{1,0:T(8,128)(2,1)S(1)}, bf16[16,192]{1,0:T(8,128)(2,1)S(1)}, u32[]{:S(2)}, u32[]{:S(2)}) %collective-permute-start.6) | collective-permute-done | bytes 6176 | tf_op jit(solution)/shard_map/ppermute | solution.py:15
  23.4 0.7 gather_fusion
  24.1 0.0 copy-start.4
  24.1 0.0 copy-start.1
  24.1 1.1 broadcast_multiply_fusion.1
  25.2 7.7 %all-to-all-start = ((bf16[32,64,192]{2,1,0:T(8,128)(2,1)}), bf16[32,64,192]{2,1,0:T(8,128)(2,1)}, u32[]{:S(2)}, u32[]{:S(2)}) async-start(bf16[32,64,192]{2,1,0:T(8,128)(2,1)} %broadcast_multiply_fusion.1), calls=%async_computation | async-start | bytes 2097152 | tf_op jit(solution)/shard_map/all_to_all | solution.py:29
  32.9 0.1 copy.18
  33.0 0.1 reshape.62
  33.8 0.7 copy.29
  34.4 1.3 %dynamic_slice.11 = f32[1]{0:T(128)} dynamic-slice(f32[1024]{0:T(1024)} %param.22, s32[]{:T(128)S(6)} %select_n.104), dynamic_slice_sizes={1} | dynamic-slice | bytes 12 | tf_op jit(solution)/shard_map/jit(dynamic_index_in_dim)/dynamic_slice | solution.py:62
  35.7 13.3 %all-to-all-done = bf16[32,64,192]{2,1,0:T(8,128)(2,1)} async-done(((bf16[32,64,192]{2,1,0:T(8,128)(2,1)}), bf16[32,64,192]{2,1,0:T(8,128)(2,1)}, u32[]{:S(2)}, u32[]{:S(2)}) %all-to-all-start) | async-done | bytes 786464 | tf_op jit(solution)/shard_map/all_to_all | solution.py:29
  49.0 0.8 dynamic-slice_bitcast_fusion.1
  49.8 0.8 gather_fusion.1
  50.6 0.1 reshape.110
  50.7 0.0 copy-start.3
  50.7 5.2 %fusion.12 = f32[16,1,192]{2,1,0:T(1,128)S(1)} fusion(bf16[16,1152,1]{1,2,0:T(2,128)(2,1)S(1)} %reshape.110, bf16[16,192,1152]{2,1,0:T(8,128)(2,1)} %param.14), kind=kOutput, calls=%fused_computation.54 | convolution fusion | flops 7077888 | bytes 7127040 | tf_op jit(solution)/shard_map/bim,bm->bi/dot_general | solution.py:43
  55.9 0.7 fusion.8
  56.6 0.3 fusion.6
  56.9 0.1 collective-permute-start.7
  57.0 3.2 %collective-permute-start.8 = (bf16[16,192]{1,0:T(8,128)(2,1)S(1)}, bf16[16,192]{1,0:T(8,128)(2,1)S(1)}, u32[]{:S(2)}, u32[]{:S(2)}) collective-permute-start(bf16[16,192]{1,0:T(8,128)(2,1)S(1)} %get-tuple-element.3), channel_id=1, source_target_pairs={{0,7},{1,0},{2,1},{3,2},{4,3},{5,4},{6,5},{7,6},{8,15},{9,8},{10,9... | collective-permute-start | bytes 18440 | tf_op jit(solution)/shard_map/ppermute | solution.py:18
  60.2 1.6 %collective-permute-done.7 = bf16[16,192]{1,0:T(8,128)(2,1)S(1)} collective-permute-done((bf16[16,192]{1,0:T(8,128)(2,1)S(1)}, bf16[16,192]{1,0:T(8,128)(2,1)S(1)}, u32[]{:S(2)}, u32[]{:S(2)}) %collective-permute-start.7) | collective-permute-done | bytes 6176 | tf_op jit(solution)/shard_map/ppermute | solution.py:15
  61.9 0.0 collective-permute-start.9
  61.9 3.2 %collective-permute-start.10 = (bf16[16,192]{1,0:T(8,128)(2,1)S(1)}, bf16[16,192]{1,0:T(8,128)(2,1)S(1)}, u32[]{:S(2)}, u32[]{:S(2)}) collective-permute-start(bf16[16,192]{1,0:T(8,128)(2,1)S(1)} %collective-permute-done.8), channel_id=1, source_target_pairs={{0,7},{1,0},{2,1},{3,2},{4,3},{5,4},{6,5},{7,6},{8,15},{9,8},{10,9... | collective-permute-start | bytes 18440 | tf_op jit(solution)/shard_map/ppermute | solution.py:18
  65.1 1.6 %collective-permute-done.9 = bf16[16,192]{1,0:T(8,128)(2,1)S(1)} collective-permute-done((bf16[16,192]{1,0:T(8,128)(2,1)S(1)}, bf16[16,192]{1,0:T(8,128)(2,1)S(1)}, u32[]{:S(2)}, u32[]{:S(2)}) %collective-permute-start.9) | collective-permute-done | bytes 6176 | tf_op jit(solution)/shard_map/ppermute | solution.py:15
  66.7 0.0 collective-permute-start.11
  66.7 0.0 collective-permute-done.10
  66.7 3.2 %collective-permute-start.12 = (bf16[16,192]{1,0:T(8,128)(2,1)S(1)}, bf16[16,192]{1,0:T(8,128)(2,1)S(1)}, u32[]{:S(2)}, u32[]{:S(2)}) collective-permute-start(bf16[16,192]{1,0:T(8,128)(2,1)S(1)} %collective-permute-done.10), channel_id=1, source_target_pairs={{0,7},{1,0},{2,1},{3,2},{4,3},{5,4},{6,5},{7,6},{8,15},{9,8},{10,9... | collective-permute-start | bytes 18440 | tf_op jit(solution)/shard_map/ppermute | solution.py:18
  70.0 1.6 %collective-permute-done.11 = bf16[16,192]{1,0:T(8,128)(2,1)S(1)} collective-permute-done((bf16[16,192]{1,0:T(8,128)(2,1)S(1)}, bf16[16,192]{1,0:T(8,128)(2,1)S(1)}, u32[]{:S(2)}, u32[]{:S(2)}) %collective-permute-start.11) | collective-permute-done | bytes 6176 | tf_op jit(solution)/shard_map/ppermute | solution.py:15
  71.6 0.0 collective-permute-start.13
  71.6 0.0 collective-permute-done.12
  71.6 4.8 %collective-permute-done.13 = bf16[16,192]{1,0:T(8,128)(2,1)S(1)} collective-permute-done((bf16[16,192]{1,0:T(8,128)(2,1)S(1)}, bf16[16,192]{1,0:T(8,128)(2,1)S(1)}, u32[]{:S(2)}, u32[]{:S(2)}) %collective-permute-start.13) | collective-permute-done | bytes 6176 | tf_op jit(solution)/shard_map/ppermute | solution.py:15
  76.4 0.7 gather_fusion.2
  77.1 0.0 copy-start.2
  77.2 0.0 copy-start.7
  77.2 0.0 copy-start.5
  77.2 1.1 broadcast_multiply_fusion
  78.3 5.0 %all-to-all-start.1 = ((bf16[32,64,192]{2,1,0:T(8,128)(2,1)}), bf16[32,64,192]{2,1,0:T(8,128)(2,1)S(1)}, u32[]{:S(2)}, u32[]{:S(2)}) async-start(bf16[32,64,192]{2,1,0:T(8,128)(2,1)} %broadcast_multiply_fusion), calls=%async_computation.1 | async-start | bytes 2097152 | tf_op jit(solution)/shard_map/all_to_all | solution.py:29
  83.4 0.1 copy.19
  83.5 0.6 dynamic-slice
  84.8 14.8 %all-to-all-done.1 = bf16[32,64,192]{2,1,0:T(8,128)(2,1)S(1)} async-done(((bf16[32,64,192]{2,1,0:T(8,128)(2,1)}), bf16[32,64,192]{2,1,0:T(8,128)(2,1)S(1)}, u32[]{:S(2)}, u32[]{:S(2)}) %all-to-all-start.1) | async-done | bytes 786464 | tf_op jit(solution)/shard_map/all_to_all | solution.py:29
  99.6 0.8 gather_fusion.3
  100.4 0.1 reshape.112
  100.5 5.2 %fusion.13 = f32[16,1,192]{2,1,0:T(1,128)S(1)} fusion(bf16[16,1152,1]{1,2,0:T(2,128)(2,1)S(1)} %reshape.112, bf16[16,192,1152]{2,1,0:T(8,128)(2,1)} %param.14), kind=kOutput, calls=%fused_computation.55 | convolution fusion | flops 7077888 | bytes 7127040 | tf_op jit(solution)/shard_map/bim,bm->bi/dot_general | solution.py:43
  105.7 0.7 fusion.9
  106.3 0.3 fusion.4
  106.7 0.8 gather_fusion.4
  107.4 0.1 multiply_reduce_fusion
  107.6 0.2 fusion
  107.7 14.2 %all-reduce = f32[64]{0:T(128)S(1)} all-reduce(f32[64]{0:T(128)S(1)} %fusion), channel_id=2, replica_groups=mesh['dom'=32,'blk'=8] {'blk'}, use_global_device_ids=true, to_apply=%region_1.2.clone | all-reduce | flops 64 | bytes 512
  121.9 0.6 dynamic-slice.1
  (39 shorter events, 0.2 us)
Async XLA Ops:
  0.6 8.1 %collective-permute-start = (bf16[16,192]{1,0:T(8,128)(2,1)}, bf16[16,192]{1,0:T(8,128)(2,1)S(1)}, u32[]{:S(2)}, u32[]{:S(2)}) collective-permute-start(bf16[16,192]{1,0:T(8,128)(2,1)} %param.13), channel_id=1, source_target_pairs={{0,1},{1,2},{2,3},{3,4},{4,5},{5,6},{6,7},{7,0},{8,9},{9,10},{10,1... | collective-permute-start | bytes 18440 | tf_op jit(solution)/shard_map/ppermute | solution.py:15
  2.6 6.2 %collective-permute-start.1 = (bf16[16,192]{1,0:T(8,128)(2,1)}, bf16[16,192]{1,0:T(8,128)(2,1)S(1)}, u32[]{:S(2)}, u32[]{:S(2)}) collective-permute-start(bf16[16,192]{1,0:T(8,128)(2,1)} %param.13), channel_id=1, source_target_pairs={{0,7},{1,0},{2,1},{3,2},{4,3},{5,4},{6,5},{7,6},{8,15},{9,8},{10,9... | collective-permute-start | bytes 18440 | tf_op jit(solution)/shard_map/ppermute | solution.py:18
  8.7 4.9 %collective-permute-start.2 = (bf16[16,192]{1,0:T(8,128)(2,1)S(1)}, bf16[16,192]{1,0:T(8,128)(2,1)S(1)}, u32[]{:S(2)}, u32[]{:S(2)}) collective-permute-start(bf16[16,192]{1,0:T(8,128)(2,1)S(1)} %collective-permute-done), channel_id=1, source_target_pairs={{0,1},{1,2},{2,3},{3,4},{4,5},{5,6},{6,7},{7,0},{8,9},{9,10},{10,1... | collective-permute-start | bytes 18440 | tf_op jit(solution)/shard_map/ppermute | solution.py:15
  8.8 4.8 %collective-permute-start.3 = (bf16[16,192]{1,0:T(8,128)(2,1)S(1)}, bf16[16,192]{1,0:T(8,128)(2,1)S(1)}, u32[]{:S(2)}, u32[]{:S(2)}) collective-permute-start(bf16[16,192]{1,0:T(8,128)(2,1)S(1)} %collective-permute-done.1), channel_id=1, source_target_pairs={{0,7},{1,0},{2,1},{3,2},{4,3},{5,4},{6,5},{7,6},{8,15},{9,8},{10,9... | collective-permute-start | bytes 18440 | tf_op jit(solution)/shard_map/ppermute | solution.py:18
  13.6 4.9 %collective-permute-start.4 = (bf16[16,192]{1,0:T(8,128)(2,1)S(1)}, bf16[16,192]{1,0:T(8,128)(2,1)S(1)}, u32[]{:S(2)}, u32[]{:S(2)}) collective-permute-start(bf16[16,192]{1,0:T(8,128)(2,1)S(1)} %collective-permute-done.2), channel_id=1, source_target_pairs={{0,1},{1,2},{2,3},{3,4},{4,5},{5,6},{6,7},{7,0},{8,9},{9,10},{10,1... | collective-permute-start | bytes 18440 | tf_op jit(solution)/shard_map/ppermute | solution.py:15
  13.6 4.9 %collective-permute-start.5 = (bf16[16,192]{1,0:T(8,128)(2,1)S(1)}, bf16[16,192]{1,0:T(8,128)(2,1)S(1)}, u32[]{:S(2)}, u32[]{:S(2)}) collective-permute-start(bf16[16,192]{1,0:T(8,128)(2,1)S(1)} %collective-permute-done.3), channel_id=1, source_target_pairs={{0,7},{1,0},{2,1},{3,2},{4,3},{5,4},{6,5},{7,6},{8,15},{9,8},{10,9... | collective-permute-start | bytes 18440 | tf_op jit(solution)/shard_map/ppermute | solution.py:18
  18.5 4.9 %collective-permute-start.6 = (bf16[16,192]{1,0:T(8,128)(2,1)S(1)}, bf16[16,192]{1,0:T(8,128)(2,1)S(1)}, u32[]{:S(2)}, u32[]{:S(2)}) collective-permute-start(bf16[16,192]{1,0:T(8,128)(2,1)S(1)} %collective-permute-done.4), channel_id=1, source_target_pairs={{0,1},{1,2},{2,3},{3,4},{4,5},{5,6},{6,7},{7,0},{8,9},{9,10},{10,1... | collective-permute-start | bytes 18440 | tf_op jit(solution)/shard_map/ppermute | solution.py:15
  24.1 8.8 %copy-start.4 = (s32[16,6]{0,1:T(8,128)S(1)}, s32[16,6]{0,1:T(8,128)}, u32[]{:S(2)}) copy-start(s32[16,6]{0,1:T(8,128)} %param.16) | copy-start | bytes 1156
  24.1 9.7 %copy-start.1 = (bf16[192,3072]{1,0:T(8,128)(2,1)S(1)}, bf16[192,3072]{1,0:T(8,128)(2,1)}, u32[]{:S(2)}) copy-start(bf16[192,3072]{1,0:T(8,128)(2,1)} %param.15) | copy-start | bytes 3538948
  25.2 23.8 %all-to-all-start = ((bf16[32,64,192]{2,1,0:T(8,128)(2,1)}), bf16[32,64,192]{2,1,0:T(8,128)(2,1)}, u32[]{:S(2)}, u32[]{:S(2)}) async-start(bf16[32,64,192]{2,1,0:T(8,128)(2,1)} %broadcast_multiply_fusion.1), calls=%async_computation | async-start | bytes 2097152 | tf_op jit(solution)/shard_map/all_to_all | solution.py:29
  50.7 5.2 %copy-start.3 = (bf16[16,192]{1,0:T(8,128)(2,1)S(1)}, bf16[16,192]{1,0:T(8,128)(2,1)}, u32[]{:S(2)}) copy-start(bf16[16,192]{1,0:T(8,128)(2,1)} %param.12) | copy-start | bytes 18436
  56.9 4.9 %collective-permute-start.7 = (bf16[16,192]{1,0:T(8,128)(2,1)S(1)}, bf16[16,192]{1,0:T(8,128)(2,1)S(1)}, u32[]{:S(2)}, u32[]{:S(2)}) collective-permute-start(bf16[16,192]{1,0:T(8,128)(2,1)S(1)} %get-tuple-element.3), channel_id=1, source_target_pairs={{0,1},{1,2},{2,3},{3,4},{4,5},{5,6},{6,7},{7,0},{8,9},{9,10},{10,1... | collective-permute-start | bytes 18440 | tf_op jit(solution)/shard_map/ppermute | solution.py:15
  57.0 4.9 %collective-permute-start.8 = (bf16[16,192]{1,0:T(8,128)(2,1)S(1)}, bf16[16,192]{1,0:T(8,128)(2,1)S(1)}, u32[]{:S(2)}, u32[]{:S(2)}) collective-permute-start(bf16[16,192]{1,0:T(8,128)(2,1)S(1)} %get-tuple-element.3), channel_id=1, source_target_pairs={{0,7},{1,0},{2,1},{3,2},{4,3},{5,4},{6,5},{7,6},{8,15},{9,8},{10,9... | collective-permute-start | bytes 18440 | tf_op jit(solution)/shard_map/ppermute | solution.py:18
  61.9 4.9 %collective-permute-start.9 = (bf16[16,192]{1,0:T(8,128)(2,1)S(1)}, bf16[16,192]{1,0:T(8,128)(2,1)S(1)}, u32[]{:S(2)}, u32[]{:S(2)}) collective-permute-start(bf16[16,192]{1,0:T(8,128)(2,1)S(1)} %collective-permute-done.7), channel_id=1, source_target_pairs={{0,1},{1,2},{2,3},{3,4},{4,5},{5,6},{6,7},{7,0},{8,9},{9,10},{10,1... | collective-permute-start | bytes 18440 | tf_op jit(solution)/shard_map/ppermute | solution.py:15
  61.9 4.9 %collective-permute-start.10 = (bf16[16,192]{1,0:T(8,128)(2,1)S(1)}, bf16[16,192]{1,0:T(8,128)(2,1)S(1)}, u32[]{:S(2)}, u32[]{:S(2)}) collective-permute-start(bf16[16,192]{1,0:T(8,128)(2,1)S(1)} %collective-permute-done.8), channel_id=1, source_target_pairs={{0,7},{1,0},{2,1},{3,2},{4,3},{5,4},{6,5},{7,6},{8,15},{9,8},{10,9... | collective-permute-start | bytes 18440 | tf_op jit(solution)/shard_map/ppermute | solution.py:18
  66.7 4.9 %collective-permute-start.11 = (bf16[16,192]{1,0:T(8,128)(2,1)S(1)}, bf16[16,192]{1,0:T(8,128)(2,1)S(1)}, u32[]{:S(2)}, u32[]{:S(2)}) collective-permute-start(bf16[16,192]{1,0:T(8,128)(2,1)S(1)} %collective-permute-done.9), channel_id=1, source_target_pairs={{0,1},{1,2},{2,3},{3,4},{4,5},{5,6},{6,7},{7,0},{8,9},{9,10},{10,1... | collective-permute-start | bytes 18440 | tf_op jit(solution)/shard_map/ppermute | solution.py:15
  66.7 4.9 %collective-permute-start.12 = (bf16[16,192]{1,0:T(8,128)(2,1)S(1)}, bf16[16,192]{1,0:T(8,128)(2,1)S(1)}, u32[]{:S(2)}, u32[]{:S(2)}) collective-permute-start(bf16[16,192]{1,0:T(8,128)(2,1)S(1)} %collective-permute-done.10), channel_id=1, source_target_pairs={{0,7},{1,0},{2,1},{3,2},{4,3},{5,4},{6,5},{7,6},{8,15},{9,8},{10,9... | collective-permute-start | bytes 18440 | tf_op jit(solution)/shard_map/ppermute | solution.py:18
  71.6 4.9 %collective-permute-start.13 = (bf16[16,192]{1,0:T(8,128)(2,1)S(1)}, bf16[16,192]{1,0:T(8,128)(2,1)S(1)}, u32[]{:S(2)}, u32[]{:S(2)}) collective-permute-start(bf16[16,192]{1,0:T(8,128)(2,1)S(1)} %collective-permute-done.11), channel_id=1, source_target_pairs={{0,1},{1,2},{2,3},{3,4},{4,5},{5,6},{6,7},{7,0},{8,9},{9,10},{10,1... | collective-permute-start | bytes 18440 | tf_op jit(solution)/shard_map/ppermute | solution.py:15
  77.1 6.2 %copy-start.2 = (bf16[128,192]{0,1:T(8,128)(2,1)S(1)}, bf16[128,192]{0,1:T(8,128)(2,1)}, u32[]{:S(2)}) copy-start(bf16[128,192]{0,1:T(8,128)(2,1)} %param.21) | copy-start | bytes 147460
  77.2 6.3 %copy-start.7 = (u32[256]{0:T(256)S(1)}, u32[256]{0:T(256)}, u32[]{:S(2)}) copy-start(u32[256]{0:T(256)} %constant.109) | copy-start | bytes 3076
  77.2 7.6 %copy-start.5 = (s32[128]{0:T(128)S(1)}, s32[128]{0:T(128)}, u32[]{:S(2)}) copy-start(s32[128]{0:T(128)} %param.19) | copy-start | bytes 1540
  78.3 21.3 %all-to-all-start.1 = ((bf16[32,64,192]{2,1,0:T(8,128)(2,1)}), bf16[32,64,192]{2,1,0:T(8,128)(2,1)S(1)}, u32[]{:S(2)}, u32[]{:S(2)}) async-start(bf16[32,64,192]{2,1,0:T(8,128)(2,1)} %broadcast_multiply_fusion), calls=%async_computation.1 | async-start | bytes 2097152 | tf_op jit(solution)/shard_map/all_to_all | solution.py:29
  105.7 1.9 %copy-start.6 = (s32[128]{0:T(128)S(1)}, s32[128]{0:T(128)}, u32[]{:S(2)}) copy-start(s32[128]{0:T(128)} %param.20) | copy-start | bytes 1540
  106.7 15.8 %copy-start = (f32[16,1,192]{2,0,1:T(8,128)}, f32[16,1,192]{2,0,1:T(8,128)S(1)}, u32[]{:S(2)}) copy-start(f32[16,1,192]{2,0,1:T(8,128)S(1)} %copy.43) | copy-start | bytes 36868
